TPU v7x, 512 devices: a whole 4x4x16 slice. The times are simulated.
512 devices in a mesh: dp: 8 (over z_lo), ctx: 64 (over x, z_hi, y, core).
Axes of the slice: x: 4, y: 4, z: 16 (z_hi: 2, z_lo: 8; z = z_hi * 8 + z_lo), core: 2. Of those that a mesh axis runs over, the one named last changes fastest.
Arguments:
- query: bfloat16 [393216, 512], P(('dp', 'ctx')), parts along dimension 0, may hold values from -14 to 14
- key: bfloat16 [393216, 128], P(('dp', 'ctx')), parts along dimension 0, may hold values from -12 to 12
- value: bfloat16 [393216, 128], P(('dp', 'ctx')), parts along dimension 0, may hold values from -6 to 6
- d_out: bfloat16 [393216, 512], P(('dp', 'ctx')), parts along dimension 0, may hold values from -6 to 6
- doc_lengths: int32 [1024], P('dp'), parts along dimension 0, may hold values from 1 to 768, 49152 in all
Outputs:
- attended: bfloat16 [393216, 512], P(('dp', 'ctx')), parts along dimension 0
- d_query: bfloat16 [393216, 512], P(('dp', 'ctx')), parts along dimension 0
- d_key: bfloat16 [393216, 128], P(('dp', 'ctx')), parts along dimension 0
- d_value: bfloat16 [393216, 128], P(('dp', 'ctx')), parts along dimension 0
There are 8 independent parts, one for each index of `dp`. A program takes and returns all parts, laid end to end along the dimension named above; each array names one. Nothing has to cross between parts.
Inputs may be any that keep to these rules, and one draw needn't show every extreme that they name: `doc_lengths`: the lengths of one session sum to 49152, and one of them is exactly 768.
All inputs are finite; a program needn't handle non-finite values.
Results may differ from a plain program's by a relative error of at most 0.035.
Values may be sent and summed in bfloat16 or wider, within the bound.
A program may use at most 64 MiB of HBM per device.

v0:
```python
import math

import jax
import jax.numpy as jnp
from jax import lax
from jax.sharding import PartitionSpec as P

HD = 128
REACH = 2


masked_score = -1e30


def from_behind(value, axis, steps):
    count = lax.axis_size(axis)
    first, last = (max(0, -steps), min(count, count - steps))
    return lax.ppermute(value, axis, [(source, source + steps) for source in range(first, last)])


def doc_index(positions, doc_lengths):
    starts = jnp.cumsum(doc_lengths) - doc_lengths
    return jnp.sum((starts[None, :] <= positions[:, None]).astype(jnp.int32), axis=1) - 1


def score_block(query_heads, keys, allowed):
    scores = jnp.einsum("rhe,ke->hrk", query_heads, keys, preferred_element_type=jnp.float32) * (
        1.0 / math.sqrt(HD)
    )
    return jnp.where(allowed[None], scores, masked_score)


def row_delta(dout_heads, attended):
    summed = jnp.sum(dout_heads.astype(jnp.float32) * attended.astype(jnp.float32), axis=2)
    return jnp.transpose(summed)[:, :, None]


def backward_terms(query_heads, dout_heads, keys, values, weights, delta):
    scale = 1.0 / math.sqrt(HD)
    dprob = jnp.einsum("rhe,ke->hrk", dout_heads, values, preferred_element_type=jnp.float32)
    dscore = (weights.astype(jnp.float32) * (dprob - delta)).astype(jnp.bfloat16)
    grad_query = jnp.einsum("hrk,ke->rhe", dscore, keys, preferred_element_type=jnp.float32) * scale
    grad_key = (
        jnp.einsum("hrk,rhe->ke", dscore, query_heads, preferred_element_type=jnp.float32) * scale
    )
    grad_value = jnp.einsum("hrk,rhe->ke", weights, dout_heads, preferred_element_type=jnp.float32)
    return (grad_query, grad_key, grad_value)


def window_group(query_heads, dout_heads, keys, values, allowed):
    rows = query_heads.shape[0]
    scores = score_block(query_heads, keys, allowed)
    row_max = jnp.max(scores, axis=2, keepdims=True)
    log_total = row_max + jnp.log(jnp.sum(jnp.exp(scores - row_max), axis=2, keepdims=True))
    weights = jnp.where(allowed[None], jnp.exp(scores - log_total), 0.0).astype(jnp.bfloat16)
    attended = jnp.einsum(
        "hrk,ke->rhe", weights, values, preferred_element_type=jnp.float32
    ).astype(jnp.bfloat16)
    delta = row_delta(dout_heads, attended)
    grad_query, grad_key, grad_value = backward_terms(
        query_heads, dout_heads, keys, values, weights, delta
    )
    tiles = keys.shape[0] // rows
    key_parts = [grad_key[index * rows : (index + 1) * rows] for index in range(tiles)]
    value_parts = [grad_value[index * rows : (index + 1) * rows] for index in range(tiles)]
    return (attended, grad_query, key_parts, value_parts)


def body(query, key, value, d_out, doc_lengths):
    count = lax.axis_size("ctx")
    device = lax.axis_index("ctx")
    rows = query.shape[0] // 2
    heads = query.shape[1] // HD
    group_size = 2
    local = jnp.concatenate([key, value], axis=1)
    offsets = list(range(-REACH, 0)) + list(range(1, REACH + 1))
    pieces = {0: local}
    received = {}
    for offset in offsets:
        if offset == 1:
            both_blocks = from_behind(local, "ctx", -1)
            received[1] = both_blocks[rows:]
            folded = both_blocks[:rows]
        else:
            sent = local[:rows] if offset < 0 else local[rows:]
            received[offset] = from_behind(sent, "ctx", -offset)
    empty_half = jnp.zeros((rows, 2 * HD), local.dtype)
    for offset in offsets:
        if offset < 0:
            pieces[offset] = jnp.concatenate([received[offset], empty_half], axis=0)
        elif offset == 1:
            pieces[offset] = jnp.concatenate([folded, received[offset]], axis=0)
        else:
            pieces[offset] = jnp.concatenate([empty_half, received[offset]], axis=0)
    nearby = jnp.stack([pieces[offset] for offset in range(-REACH, REACH + 1)])
    grads = jnp.zeros((2 * REACH + 1, 2 * rows, 2 * HD), jnp.float32)
    line = jnp.arange(rows, dtype=jnp.int32)
    attended_rows, grad_query_rows = ([], [])
    for slot in range(2):
        block_id = device if slot == 0 else 2 * count - 1 - device
        query_block = query[slot * rows : (slot + 1) * rows].reshape(rows, heads, HD)
        dout_block = d_out[slot * rows : (slot + 1) * rows].reshape(rows, heads, HD)
        query_pos = block_id * rows + line
        query_doc = doc_index(query_pos, doc_lengths)
        key_tiles, value_tiles, allowed_tiles, live, places = ([], [], [], [], [])
        for back in range(REACH, -1, -1):
            source = block_id - back
            clamped = jnp.maximum(source, 0)
            owner = jnp.where(clamped < count, clamped, 2 * count - 1 - clamped)
            place = owner - device + REACH
            start = jnp.where(clamped < count, 0, rows).astype(jnp.int32)
            tile = lax.dynamic_slice(nearby, (place, start, jnp.int32(0)), (1, rows, 2 * HD))[0]
            key_pos = source * rows + line
            key_doc = doc_index(key_pos, doc_lengths)
            allowed_tiles.append(
                (key_pos[None, :] <= query_pos[:, None]) & (key_doc[None, :] == query_doc[:, None])
            )
            live.append(jnp.logical_or(back == 0, key_doc[rows - 1] == query_doc[0]))
            key_tiles.append(tile[:, :HD])
            value_tiles.append(tile[:, HD:])
            places.append((place, start))
        keys = jnp.concatenate(key_tiles, axis=0)
        values = jnp.concatenate(value_tiles, axis=0)
        allowed = jnp.concatenate(allowed_tiles, axis=1)
        attended_parts, grad_query_parts = ([], [])
        key_sums = [jnp.zeros((rows, HD), jnp.float32) for place in places]
        value_sums = [jnp.zeros((rows, HD), jnp.float32) for place in places]
        for first in range(0, heads, group_size):
            query_heads = query_block[:, first : first + group_size]
            dout_heads = dout_block[:, first : first + group_size]
            attended, grad_query, key_parts, value_parts = window_group(
                query_heads, dout_heads, keys, values, allowed
            )
            attended_parts.append(attended)
            grad_query_parts.append(grad_query)
            key_sums = [total + part for total, part in zip(key_sums, key_parts)]
            value_sums = [total + part for total, part in zip(value_sums, value_parts)]
        attended_rows.append(jnp.concatenate(attended_parts, axis=1).reshape(rows, heads * HD))
        grad_query_rows.append(
            jnp.concatenate(grad_query_parts, axis=1).reshape(rows, heads * HD).astype(jnp.bfloat16)
        )
        for index in range(len(places)):
            place, start = places[index]
            update = jnp.concatenate([key_sums[index], value_sums[index]], axis=1)[None]
            current = lax.dynamic_slice(grads, (place, start, jnp.int32(0)), (1, rows, 2 * HD))
            grads = lax.dynamic_update_slice(grads, current + update, (place, start, jnp.int32(0)))
    total = grads[REACH]
    lower = total[:rows]
    upper = total[rows:]
    for offset in offsets:
        if offset == 1:
            moved_both = from_behind(grads[REACH + 1], "ctx", 1)
            lower = lower + moved_both[:rows]
            upper = upper + moved_both[rows:]
        else:
            half = 0 if offset < 0 else 1
            moved = from_behind(
                grads[REACH + offset][half * rows : (half + 1) * rows], "ctx", offset
            )
            if offset < 0:
                lower = lower + moved
            else:
                upper = upper + moved
    total = jnp.concatenate([lower, upper], axis=0)
    attended_all = jnp.concatenate(attended_rows, axis=0)
    grad_query_all = jnp.concatenate(grad_query_rows, axis=0)
    return (
        attended_all,
        grad_query_all,
        total[:, :HD].astype(jnp.bfloat16),
        total[:, HD:].astype(jnp.bfloat16),
    )


def solution(mesh):
    placed = (
        P(("dp", "ctx"), None),
        P(("dp", "ctx"), None),
        P(("dp", "ctx"), None),
        P(("dp", "ctx"), None),
        P("dp"),
    )
    return jax.shard_map(
        body,
        mesh=mesh,
        in_specs=placed,
        out_specs=(
            P(("dp", "ctx"), None),
            P(("dp", "ctx"), None),
            P(("dp", "ctx"), None),
            P(("dp", "ctx"), None),
        ),
        check_vma=False,
    )
```

profile of v0, /device:TPU:227, one launch (start us, length us, event | category | flops | bytes accessed | tf_op | source)
XLA Modules:
  0.0 163.2 jit_solution(15293366805107848099)
XLA Ops:
  0.6 1.0 constant_dynamic-update-slice_fusion.1
  1.7 1.0 constant_dynamic-update-slice_fusion
  2.7 0.7 fusion.69
  3.4 3.8 %collective-permute-start.1 = (bf16[384,256]{1,0:T(8,128)(2,1)}, bf16[384,256]{1,0:T(8,128)(2,1)}, u32[]{:S(2)}, u32[]{:S(2)}) collective-permute-start(bf16[384,256]{1,0:T(8,128)(2,1)} %get-tuple-element.60), channel_id=1, source_target_pairs={{0,1},{1,2},{2,3},{3,4},{4,5},{5,6},{6,7},{7,8},{8,9},{9,10},{10,1... | collective-permute-start | bytes 589832 | tf_op jit(solution)/shard_map/ppermute | solution.py:18
  7.1 3.2 %collective-permute-start = (bf16[384,256]{1,0:T(8,128)(2,1)}, bf16[384,256]{1,0:T(8,128)(2,1)}, u32[]{:S(2)}, u32[]{:S(2)}) collective-permute-start(bf16[384,256]{1,0:T(8,128)(2,1)} %get-tuple-element.60), channel_id=1, source_target_pairs={{0,2},{1,3},{2,4},{3,5},{4,6},{5,7},{6,8},{7,9},{8,10},{9,11},{10,... | collective-permute-start | bytes 589832 | tf_op jit(solution)/shard_map/ppermute | solution.py:18
  10.3 1.9 %collective-permute-start.2 = (bf16[768,256]{1,0:T(8,128)(2,1)S(1)}, bf16[768,256]{1,0:T(8,128)(2,1)}, u32[]{:S(2)}, u32[]{:S(2)}) collective-permute-start(bf16[768,256]{1,0:T(8,128)(2,1)S(1)} %constant_dynamic-update-slice_fusion), channel_id=1, source_target_pairs={{1,0},{2,1},{3,2},{4,3},{5,4},{6,5},{7,6},{8,7},{9,8},{10,9},{11,1... | collective-permute-start | bytes 1179656 | tf_op jit(solution)/shard_map/ppermute | solution.py:18
  12.3 13.8 %collective-permute-start.3 = (bf16[384,256]{1,0:T(8,128)(2,1)S(1)}, bf16[384,256]{1,0:T(8,128)(2,1)}, u32[]{:S(2)}, u32[]{:S(2)}) collective-permute-start(bf16[384,256]{1,0:T(8,128)(2,1)S(1)} %get-tuple-element.59), channel_id=1, source_target_pairs={{2,0},{3,1},{4,2},{5,3},{6,4},{7,5},{8,6},{9,7},{10,8},{11,9},{12,... | collective-permute-start | bytes 589832 | tf_op jit(solution)/shard_map/ppermute | solution.py:18
  26.2 0.8 copy.97
  27.2 0.7 sub.185
  27.9 1.2 fusion.67
  29.1 0.7 convert_reduce_fusion.5
  29.9 0.6 compare_and_fusion.2
  32.3 9.9 %collective-permute-done = bf16[384,256]{1,0:T(8,128)(2,1)} collective-permute-done((bf16[384,256]{1,0:T(8,128)(2,1)}, bf16[384,256]{1,0:T(8,128)(2,1)}, u32[]{:S(2)}, u32[]{:S(2)}) %collective-permute-start) | collective-permute-done | bytes 196640 | tf_op jit(solution)/shard_map/ppermute | solution.py:18
  42.2 1.0 bitcast_dynamic-update-slice_fusion.4
  43.2 1.0 bitcast_dynamic-update-slice_fusion.3
  44.2 1.0 bitcast_dynamic-update-slice_fusion.1
  45.2 2.1 %collective-permute-done.3 = bf16[384,256]{1,0:T(8,128)(2,1)} collective-permute-done((bf16[384,256]{1,0:T(8,128)(2,1)S(1)}, bf16[384,256]{1,0:T(8,128)(2,1)}, u32[]{:S(2)}, u32[]{:S(2)}) %collective-permute-start.3) | collective-permute-done | bytes 196640 | tf_op jit(solution)/shard_map/ppermute | solution.py:18
  47.3 1.0 bitcast_dynamic-update-slice_fusion
  48.5 0.8 fusion.79
  49.3 0.8 fusion.78
  51.1 1.4 select_convert_fusion.3
  52.5 0.7 convolution_bitcast_fusion.9
  54.2 0.6 fusion.16
  55.3 0.7 fusion.23
  56.0 0.7 convolution_bitcast_fusion.8
  56.7 0.6 fusion.17
  57.8 0.7 fusion.22
  58.5 0.8 fusion.77
  59.3 0.8 fusion.76
  61.1 1.6 select_convert_fusion.1
  62.7 0.7 convolution_bitcast_fusion.5
  64.4 0.6 fusion.18
  65.4 0.7 fusion.21
  66.2 0.7 convolution_bitcast_fusion.4
  66.8 0.6 fusion.19
  67.5 0.7 fusion.20
  69.3 1.1 slice_bitcast_fusion.4
  70.5 1.9 %collective-permute-start.6 = (f32[768,256]{0,1:T(8,128)S(1)}, f32[768,256]{0,1:T(8,128)}, u32[]{:S(2)}, u32[]{:S(2)}) collective-permute-start(f32[768,256]{0,1:T(8,128)S(1)} %slice_bitcast_fusion), channel_id=1, source_target_pairs={{0,1},{1,2},{2,3},{3,4},{4,5},{5,6},{6,7},{7,8},{8,9},{9,10},{10,1... | collective-permute-start | bytes 2359304 | tf_op jit(solution)/shard_map/ppermute | solution.py:18
  72.5 25.5 %collective-permute-start.4 = (f32[384,256]{0,1:T(8,128)}, f32[384,256]{0,1:T(8,128)}, u32[]{:S(2)}, u32[]{:S(2)}) collective-permute-start(f32[384,256]{0,1:T(8,128)} %get-tuple-element.28), channel_id=1, source_target_pairs={{2,0},{3,1},{4,2},{5,3},{6,4},{7,5},{8,6},{9,7},{10,8},{11,9},{12,... | collective-permute-start | bytes 1179656 | tf_op jit(solution)/shard_map/ppermute | solution.py:18
  97.9 1.9 %collective-permute-start.7 = (f32[384,256]{0,1:T(8,128)}, f32[384,256]{0,1:T(8,128)}, u32[]{:S(2)}, u32[]{:S(2)}) collective-permute-start(f32[384,256]{0,1:T(8,128)} %get-tuple-element.29), channel_id=1, source_target_pairs={{0,2},{1,3},{2,4},{3,5},{4,6},{5,7},{6,8},{7,9},{8,10},{9,11},{10,... | collective-permute-start | bytes 1179656 | tf_op jit(solution)/shard_map/ppermute | solution.py:18
  99.9 3.2 %collective-permute-start.5 = (f32[384,256]{0,1:T(8,128)S(1)}, f32[384,256]{0,1:T(8,128)}, u32[]{:S(2)}, u32[]{:S(2)}) collective-permute-start(f32[384,256]{0,1:T(8,128)S(1)} %get-tuple-element.30), channel_id=1, source_target_pairs={{1,0},{2,1},{3,2},{4,3},{5,4},{6,5},{7,6},{8,7},{9,8},{10,9},{11,1... | collective-permute-start | bytes 1179656 | tf_op jit(solution)/shard_map/ppermute | solution.py:18
  104.5 0.9 pad_maximum_fusion
  105.4 0.9 pad_maximum_fusion.1
  106.3 29.6 %collective-permute-done.4 = f32[384,256]{0,1:T(8,128)} collective-permute-done((f32[384,256]{0,1:T(8,128)}, f32[384,256]{0,1:T(8,128)}, u32[]{:S(2)}, u32[]{:S(2)}) %collective-permute-start.4) | collective-permute-done | bytes 393248 | tf_op jit(solution)/shard_map/ppermute | solution.py:18
  136.0 23.6 %collective-permute-done.7 = f32[384,256]{0,1:T(8,128)} collective-permute-done((f32[384,256]{0,1:T(8,128)}, f32[384,256]{0,1:T(8,128)}, u32[]{:S(2)}, u32[]{:S(2)}) %collective-permute-start.7) | collective-permute-done | bytes 393248 | tf_op jit(solution)/shard_map/ppermute | solution.py:18
  159.6 1.8 %slice_add_fusion.1 = (bf16[384,256]{0,1:T(8,128)(2,1)S(1)}, bf16[384,256]{0,1:T(8,128)(2,1)S(1)}) fusion(f32[768,256]{0,1:T(8,128)} %collective-permute-done.6, f32[384,256]{0,1:T(8,128)} %collective-permute-done.5, f32[384,256]{0,1:T(8,128)} %collective-permute-done.4, f32[5,768,256]{1,2,0:T(8,128)} %copy-done, f32[384,256]{0,1:T(8,128)} %collective-permute-done.7), kind=kLoop, calls=%fused_computation.84 | loop fusion | flops 688128 | bytes 3145728 | tf_op jit(solution)/shard_map/add | solution.py:153
  161.6 0.8 copy.143
  162.4 0.8 copy.142
  (70 shorter events, 10.3 us)
Async XLA Ops:
  0.6 28.4 %copy-start.1 = (bf16[768,512]{1,0:T(8,128)(2,1)S(1)}, bf16[768,512]{1,0:T(8,128)(2,1)}, u32[]{:S(2)}) copy-start(bf16[768,512]{1,0:T(8,128)(2,1)} %param.8) | copy-start | bytes 2359300
  3.4 39.8 %collective-permute-start.1 = (bf16[384,256]{1,0:T(8,128)(2,1)}, bf16[384,256]{1,0:T(8,128)(2,1)}, u32[]{:S(2)}, u32[]{:S(2)}) collective-permute-start(bf16[384,256]{1,0:T(8,128)(2,1)} %get-tuple-element.60), channel_id=1, source_target_pairs={{0,1},{1,2},{2,3},{3,4},{4,5},{5,6},{6,7},{7,8},{8,9},{9,10},{10,1... | collective-permute-start | bytes 589832 | tf_op jit(solution)/shard_map/ppermute | solution.py:18
  7.1 35.1 %collective-permute-start = (bf16[384,256]{1,0:T(8,128)(2,1)}, bf16[384,256]{1,0:T(8,128)(2,1)}, u32[]{:S(2)}, u32[]{:S(2)}) collective-permute-start(bf16[384,256]{1,0:T(8,128)(2,1)} %get-tuple-element.60), channel_id=1, source_target_pairs={{0,2},{1,3},{2,4},{3,5},{4,6},{5,7},{6,8},{7,9},{8,10},{9,11},{10,... | collective-permute-start | bytes 589832 | tf_op jit(solution)/shard_map/ppermute | solution.py:18
  10.3 33.9 %collective-permute-start.2 = (bf16[768,256]{1,0:T(8,128)(2,1)S(1)}, bf16[768,256]{1,0:T(8,128)(2,1)}, u32[]{:S(2)}, u32[]{:S(2)}) collective-permute-start(bf16[768,256]{1,0:T(8,128)(2,1)S(1)} %constant_dynamic-update-slice_fusion), channel_id=1, source_target_pairs={{1,0},{2,1},{3,2},{4,3},{5,4},{6,5},{7,6},{8,7},{9,8},{10,9},{11,1... | collective-permute-start | bytes 1179656 | tf_op jit(solution)/shard_map/ppermute | solution.py:18
  12.3 35.0 %collective-permute-start.3 = (bf16[384,256]{1,0:T(8,128)(2,1)S(1)}, bf16[384,256]{1,0:T(8,128)(2,1)}, u32[]{:S(2)}, u32[]{:S(2)}) collective-permute-start(bf16[384,256]{1,0:T(8,128)(2,1)S(1)} %get-tuple-element.59), channel_id=1, source_target_pairs={{2,0},{3,1},{4,2},{5,3},{6,4},{7,5},{8,6},{9,7},{10,8},{11,9},{12,... | collective-permute-start | bytes 589832 | tf_op jit(solution)/shard_map/ppermute | solution.py:18
  69.2 34.3 %copy-start = (f32[5,768,256]{1,2,0:T(8,128)}, f32[5,768,256]{1,2,0:T(8,128)S(1)}, u32[]{:S(2)}) copy-start(f32[5,768,256]{1,2,0:T(8,128)S(1)} %fusion.49) | copy-start | bytes 11796484
  70.5 89.2 %collective-permute-start.6 = (f32[768,256]{0,1:T(8,128)S(1)}, f32[768,256]{0,1:T(8,128)}, u32[]{:S(2)}, u32[]{:S(2)}) collective-permute-start(f32[768,256]{0,1:T(8,128)S(1)} %slice_bitcast_fusion), channel_id=1, source_target_pairs={{0,1},{1,2},{2,3},{3,4},{4,5},{5,6},{6,7},{7,8},{8,9},{9,10},{10,1... | collective-permute-start | bytes 2359304 | tf_op jit(solution)/shard_map/ppermute | solution.py:18
  72.5 63.5 %collective-permute-start.4 = (f32[384,256]{0,1:T(8,128)}, f32[384,256]{0,1:T(8,128)}, u32[]{:S(2)}, u32[]{:S(2)}) collective-permute-start(f32[384,256]{0,1:T(8,128)} %get-tuple-element.28), channel_id=1, source_target_pairs={{2,0},{3,1},{4,2},{5,3},{6,4},{7,5},{8,6},{9,7},{10,8},{11,9},{12,... | collective-permute-start | bytes 1179656 | tf_op jit(solution)/shard_map/ppermute | solution.py:18
  97.9 61.7 %collective-permute-start.7 = (f32[384,256]{0,1:T(8,128)}, f32[384,256]{0,1:T(8,128)}, u32[]{:S(2)}, u32[]{:S(2)}) collective-permute-start(f32[384,256]{0,1:T(8,128)} %get-tuple-element.29), channel_id=1, source_target_pairs={{0,2},{1,3},{2,4},{3,5},{4,6},{5,7},{6,8},{7,9},{8,10},{9,11},{10,... | collective-permute-start | bytes 1179656 | tf_op jit(solution)/shard_map/ppermute | solution.py:18
  99.9 59.8 %collective-permute-start.5 = (f32[384,256]{0,1:T(8,128)S(1)}, f32[384,256]{0,1:T(8,128)}, u32[]{:S(2)}, u32[]{:S(2)}) collective-permute-start(f32[384,256]{0,1:T(8,128)S(1)} %get-tuple-element.30), channel_id=1, source_target_pairs={{1,0},{2,1},{3,2},{4,3},{5,4},{6,5},{7,6},{8,7},{9,8},{10,9},{11,1... | collective-permute-start | bytes 1179656 | tf_op jit(solution)/shard_map/ppermute | solution.py:18
where the time goes:
time: 164 us; the launch traced here: 163 us
  waiting for transfers between devices  65.3 us (40%)
  starting transfers between devices  55.2 us (34%)
  matrix products  14.9 us (9%)
  local copies, waits for them, and re-layouts  13.7 us (8%)
  other arithmetic  12.6 us (8%)
    ppermute x8, waiting for transfers between devices, from_behind(): lax.ppermute(value, axis, [(source, source + steps) for source in range(f...  65.3 us
    ppermute x8, starting transfers between devices, from_behind(): lax.ppermute(value, axis, [(source, source + steps) for source in range(f...  55.2 us
    unnamed x13, local copies, waits for them, and re-layouts  6.05 us
  transfers between devices with their start and end apart: 8, of which 4 were waited for; matrix products, arithmetic and copies ran while one was open for 7% of the time, Pallas kernels for 0%

commit v1 on v0

v1 whole, which is shorter than its diff:
```python
import math

import jax
import jax.numpy as jnp
from jax import lax
from jax.experimental import pallas as pl
from jax.experimental.pallas import tpu as pltpu
from jax.sharding import PartitionSpec as P

HD = 128
QH = 4
CH = 384
SUB = 128
WIN = 7 * SUB
OWN = 2 * CH
CHIPS = 32
MASKED = -1e30
SCALE = 1.0 / math.sqrt(HD)
SCALE2 = SCALE * math.log2(math.e)
MESH = pl.DeviceIdType.MESH
NT = (((1,), (1,)), ((), ()))
TN = (((0,), (0,)), ((), ()))
AK, AV, BK, BV, CK, CV, FK, FV, RK, RV, GA, GB, GC, GF, GR, COPIES = range(16)


def dot(a, b, dims):
    return lax.dot_general(a, b, dims, preferred_element_type=jnp.float32)


def kernel(
    q_ref, k_ref, v_ref, do_ref, len_ref,
    att_ref, dq_ref, dk_ref, dv_ref,
    kbuf, vbuf, first, acck, accv, gout, gin, gfold, relay, grelay, send, recv, fwd,
):
    d = lax.axis_index("ctx")
    c, k = d // 2, lax.rem(d, 2)
    y = lax.rem(c, 4)
    other = 1 - k
    step = 2 * k - 1
    u, w = c + step, c - step
    u2, w2 = c + 2 * step, c - 2 * step
    edge_u, edge_w = 3 * k, 3 * (1 - k)
    has_u = (u >= 0) & (u < CHIPS)
    has_w = (w >= 0) & (w < CHIPS)
    cross_u = has_u & (y == edge_u)
    cross_w = has_w & (y == edge_w)
    near_u = has_u & (y != edge_u)
    near_w = has_w & (y != edge_w)
    fold = (c == CHIPS - 1) & (k == 1)
    folded = (c == CHIPS - 1) & (k == 0)
    relay_kv = (y == edge_w + 1 - 2 * (1 - k)) & (w2 >= 0) & (w2 < CHIPS)
    relay_g = (y == edge_u + 1 - 2 * k) & (u2 >= 0) & (u2 < CHIPS)

    def at(chip, core):
        return {"ctx": chip * 2 + core}

    barrier = pltpu.get_barrier_semaphore()

    def greet(when, chip, core):
        @pl.when(when)
        def _():
            pl.semaphore_signal(barrier, inc=1, device_id=at(chip, core), device_id_type=MESH)

    pl.semaphore_signal(barrier, inc=1, device_id=at(c, other), device_id_type=MESH)
    greet(has_u, u, other)
    greet(near_u, u, k)
    greet(near_w, w, k)
    greet(cross_u, u2, k)
    greet(cross_w, w2, k)

    for slot in range(2):
        rows = slice(slot * CH, (slot + 1) * CH)
        kbuf[slot, OWN:] = k_ref[rows]
        vbuf[slot, OWN:] = v_ref[rows]

    @pl.when((c == 0) & (k == 0))
    def _():
        kbuf[0, :OWN] = jnp.zeros((OWN, HD), jnp.bfloat16)
        vbuf[0, :OWN] = jnp.zeros((OWN, HD), jnp.bfloat16)

    acck[...] = jnp.zeros_like(acck)
    accv[...] = jnp.zeros_like(accv)

    lens = jnp.broadcast_to(len_ref[...], (HD, HD))
    line = lax.broadcasted_iota(jnp.int32, (HD, HD), 0)
    lane = lax.broadcasted_iota(jnp.int32, (HD, HD), 1)
    starts = jnp.sum(
        jnp.where(lane < line, lens, 0).astype(jnp.float32), axis=1, keepdims=True
    ).astype(jnp.int32)
    for slot in range(2):
        block = d if slot == 0 else 2 * (2 * CHIPS) - 1 - d
        for sub in range(3):
            pos = block * CH + sub * SUB + lane
            held = jnp.where(starts <= pos, starts, 0)
            held = jnp.max(held.astype(jnp.float32), axis=0, keepdims=True).astype(jnp.int32)
            first[slot, sub] = jnp.broadcast_to(held - (block * CH - OWN + sub * SUB), (8, HD))

    count = (
        1
        + has_u.astype(jnp.int32)
        + near_u.astype(jnp.int32)
        + near_w.astype(jnp.int32)
        + relay_kv.astype(jnp.int32)
        + relay_g.astype(jnp.int32)
    )
    pl.semaphore_wait(barrier, count)

    def remote(src, dst, which, chip, core, out=None):
        return pltpu.make_async_remote_copy(
            src_ref=src,
            dst_ref=dst,
            send_sem=send.at[which] if out is None else out,
            recv_sem=recv.at[which],
            device_id=at(chip, core),
            device_id_type=MESH,
        )

    near, far = pl.ds(CH, CH), pl.ds(0, CH)
    mine, theirs = pl.ds(k * CH, CH), pl.ds(other * CH, CH)
    send_a = [
        remote(k_ref.at[theirs], kbuf.at[other, near], AK, u, other),
        remote(v_ref.at[theirs], vbuf.at[other, near], AV, u, other),
    ]
    send_b = [
        remote(k_ref.at[mine], kbuf.at[k, far], BK, w, k),
        remote(v_ref.at[mine], vbuf.at[k, far], BV, w, k),
    ]
    send_r = [
        remote(k_ref.at[mine], relay.at[0], RK, u, k),
        remote(v_ref.at[mine], relay.at[1], RV, u, k),
    ]
    send_c = [
        remote(k_ref.at[mine], kbuf.at[k, near], CK, c, other),
        remote(v_ref.at[mine], vbuf.at[k, near], CV, c, other),
    ]
    send_f = [
        remote(kbuf.at[k, near], kbuf.at[k, far], FK, c, other),
        remote(vbuf.at[k, near], vbuf.at[k, far], FV, c, other),
    ]
    pass_on = [
        remote(relay.at[0], kbuf.at[k, far], BK, w2, k, fwd.at[0]),
        remote(relay.at[1], vbuf.at[k, far], BV, w2, k, fwd.at[1]),
    ]
    send_ga = remote(gout.at[k, 1], gin.at[0], GA, u, other)
    send_gb = remote(gout.at[k, 0], gin.at[1], GB, u, k)
    send_gfold = remote(gout.at[k, 0], gin.at[1], GB, c, other)
    send_gr = remote(gout.at[k, 0], grelay, GR, w, k)
    send_gc = remote(gout.at[other, 1], gin.at[2], GC, c, other)
    send_gf = remote(gout.at[other, 0], gfold, GF, c, other)
    pass_g = remote(grelay, gin.at[1], GB, u2, k, fwd.at[2])

    def start(when, copies):
        @pl.when(when)
        def _():
            for copy in copies:
                copy.start()

    start(has_u, send_a)
    start(cross_w, send_r)
    start(near_w, send_b)
    for copy in send_c:
        copy.start()

    @pl.when(relay_kv)
    def _():
        for come, go in zip(send_r, pass_on):
            come.wait_recv()
            go.start()

    def landed(dst, which):
        remote(dst, dst, which, c, other).wait_recv()

    def prepare(slot):
        @pl.when(slot == k)
        def _():
            @pl.when(has_u)
            def _():
                landed(kbuf.at[k, near], AK)
                landed(vbuf.at[k, near], AV)

            @pl.when(fold)
            def _():
                kbuf[1, CH:OWN] = k_ref[:CH]
                vbuf[1, CH:OWN] = v_ref[:CH]
                kbuf[1, :CH] = kbuf[0, CH:OWN]
                vbuf[1, :CH] = vbuf[0, CH:OWN]

            for copy in send_f:
                copy.start()

            @pl.when(has_u)
            def _():
                landed(kbuf.at[k, far], BK)
                landed(vbuf.at[k, far], BV)

        @pl.when(slot == other)
        def _():
            landed(kbuf.at[other, near], CK)
            landed(vbuf.at[other, near], CV)
            landed(kbuf.at[other, far], FK)
            landed(vbuf.at[other, far], FV)

    def attend(slot):
        def tile(sub, carry):
            rows = pl.ds(pl.multiple_of(slot * CH + sub * SUB, SUB), SUB)
            window = pl.ds(pl.multiple_of(sub * SUB, SUB), WIN)
            keys = kbuf[slot, window]
            values = vbuf[slot, window]
            key_line = lax.broadcasted_iota(jnp.int32, (WIN, SUB), 0)
            query_lane = lax.broadcasted_iota(jnp.int32, (WIN, SUB), 1)
            allowed = (key_line - OWN <= query_lane) & (key_line >= first[slot, sub][:1])
            bias = jnp.where(allowed, 0.0, MASKED)
            bias = jnp.concatenate([bias, bias], axis=1)
            grad_k = grad_v = None
            for pair in range(QH // 2):
                heads = [slice(h * HD, (h + 1) * HD) for h in (2 * pair, 2 * pair + 1)]
                query = jnp.concatenate([q_ref[rows, h] for h in heads], axis=0)
                dout = jnp.concatenate([do_ref[rows, h] for h in heads], axis=0)
                scores = dot(keys, query, NT) * SCALE2 + bias
                top = jnp.max(scores, axis=0, keepdims=True)
                raised = jnp.exp2(scores - top)
                total = jnp.sum(raised, axis=0, keepdims=True)
                weights = (raised * (1.0 / total)).astype(jnp.bfloat16)
                attended = dot(weights, values, TN).astype(jnp.bfloat16)
                product = dout.astype(jnp.float32) * attended.astype(jnp.float32)
                delta = lax.dot_general(
                    jnp.ones((8, HD), jnp.float32), product, NT,
                    precision=lax.Precision.HIGHEST, preferred_element_type=jnp.float32,
                )[:1]
                dprob = dot(values, dout, NT)
                dscore = (weights.astype(jnp.float32) * (dprob - delta)).astype(jnp.bfloat16)
                grad_q = (dot(dscore, keys, TN) * SCALE).astype(jnp.bfloat16)
                for half in range(2):
                    part = slice(half * SUB, (half + 1) * SUB)
                    att_ref[rows, heads[half]] = attended[part]
                    dq_ref[rows, heads[half]] = grad_q[part]
                new_k = dot(dscore, query, (((1,), (0,)), ((), ())))
                new_v = dot(weights, dout, (((1,), (0,)), ((), ())))
                grad_k = new_k if grad_k is None else grad_k + new_k
                grad_v = new_v if grad_v is None else grad_v + new_v
            acck[slot, window] = acck[slot, window] + grad_k
            accv[slot, window] = accv[slot, window] + grad_v
            return carry

        lax.fori_loop(0, 3, tile, 0)

    def give(slot):
        @pl.when(slot == other)
        def _():
            for place in range(2):
                rows = slice(place * CH, (place + 1) * CH)
                gout[other, place, :CH] = acck[other, rows].astype(jnp.bfloat16)
                gout[other, place, CH:] = accv[other, rows].astype(jnp.bfloat16)
            send_gf.start()
            send_gc.start()

        @pl.when(slot == k)
        def _():
            gout[k, 0, :CH] = acck[k, :CH].astype(jnp.bfloat16)
            gout[k, 0, CH:] = accv[k, :CH].astype(jnp.bfloat16)
            start(near_u, [send_gb])
            start(cross_u, [send_gr])
            start(fold, [send_gfold])
            send_gf.wait_recv()
            sum_k = acck[k, CH:OWN] + gfold[:CH].astype(jnp.float32)
            sum_v = accv[k, CH:OWN] + gfold[CH:].astype(jnp.float32)

            @pl.when(has_u)
            def _():
                gout[k, 1, :CH] = sum_k.astype(jnp.bfloat16)
                gout[k, 1, CH:] = sum_v.astype(jnp.bfloat16)
                send_ga.start()

            @pl.when(fold)
            def _():
                acck[0, OWN:] = acck[0, OWN:] + sum_k
                accv[0, OWN:] = accv[0, OWN:] + sum_v

    early = (y < 2).astype(jnp.int32)

    def turn(index, carry):
        slot = early + index - 2 * early * index
        prepare(slot)
        attend(slot)
        give(slot)
        return carry

    lax.fori_loop(0, 2, turn, 0)

    @pl.when(relay_g)
    def _():
        send_gr.wait_recv()
        pass_g.start()

    def add(slot, which):
        acck[slot, OWN:] = acck[slot, OWN:] + gin[which, :CH].astype(jnp.float32)
        accv[slot, OWN:] = accv[slot, OWN:] + gin[which, CH:].astype(jnp.float32)

    send_gc.wait_recv()
    add(k, 2)

    @pl.when(has_u)
    def _():
        send_ga.wait_recv()
        add(other, 0)

    @pl.when(has_w | folded)
    def _():
        send_gb.wait_recv()
        add(k, 1)

    for slot in range(2):
        rows = slice(slot * CH, (slot + 1) * CH)
        dk_ref[rows] = (acck[slot, OWN:] * SCALE).astype(jnp.bfloat16)
        dv_ref[rows] = accv[slot, OWN:].astype(jnp.bfloat16)

    def sent(when, copies):
        @pl.when(when)
        def _():
            for copy in copies:
                copy.wait_send()

    for copy in send_c + send_f + [send_gc, send_gf]:
        copy.wait_send()
    sent(has_u, send_a + [send_ga])
    sent(near_w, send_b)
    sent(cross_w, send_r)
    sent(relay_kv, pass_on)
    sent(near_u, [send_gb])
    sent(cross_u, [send_gr])
    sent(fold, [send_gfold])
    sent(relay_g, [pass_g])


def body(query, key, value, d_out, doc_lengths):
    rows, features = query.shape
    vmem = pl.BlockSpec(memory_space=pltpu.VMEM)
    bf16, f32 = jnp.bfloat16, jnp.float32
    return pl.pallas_call(
        kernel,
        out_shape=[
            jax.ShapeDtypeStruct((rows, features), bf16),
            jax.ShapeDtypeStruct((rows, features), bf16),
            jax.ShapeDtypeStruct((rows, HD), bf16),
            jax.ShapeDtypeStruct((rows, HD), bf16),
        ],
        in_specs=[vmem] * 5,
        out_specs=[vmem] * 4,
        scratch_shapes=[
            pltpu.VMEM((2, 3 * CH, HD), bf16),
            pltpu.VMEM((2, 3 * CH, HD), bf16),
            pltpu.VMEM((2, 3, 8, HD), jnp.int32),
            pltpu.VMEM((2, 3 * CH, HD), f32),
            pltpu.VMEM((2, 3 * CH, HD), f32),
            pltpu.VMEM((2, 2, 2 * CH, HD), bf16),
            pltpu.VMEM((3, 2 * CH, HD), bf16),
            pltpu.VMEM((2 * CH, HD), bf16),
            pltpu.VMEM((2, CH, HD), bf16),
            pltpu.VMEM((2 * CH, HD), bf16),
            pltpu.SemaphoreType.DMA((COPIES,)),
            pltpu.SemaphoreType.DMA((COPIES,)),
            pltpu.SemaphoreType.DMA((3,)),
        ],
        compiler_params=pltpu.CompilerParams(
            collective_id=0, has_side_effects=True, vmem_limit_bytes=48 * 2**20
        ),
        cost_estimate=pl.CostEstimate(
            flops=4_300_000_000, bytes_accessed=4_000_000, transcendentals=2_800_000
        ),
    )(query, key, value, d_out, doc_lengths.reshape(1, -1))


def solution(mesh):
    wide = P(("dp", "ctx"), None)
    return jax.shard_map(
        body,
        mesh=mesh,
        in_specs=(wide, wide, wide, wide, P("dp")),
        out_specs=(wide, wide, wide, wide),
        check_vma=False,
    )
```

time: 164 us -> 73.4 us (0.45)
  the two profiles are of different devices: /device:TPU:227 before, /device:TPU:39 now
where the time goes in v1:
time: 73.4 us; the launch traced here: 73.1 us
  Pallas kernels  64.6 us (88%)
  local copies, waits for them, and re-layouts  7.88 us (11%)
    pallas_call x1, Pallas kernels, body(): pl.pallas_call(kernel, out_shape=[jax.ShapeDtypeStruct((rows, features),...  64.6 us
    unnamed x14, local copies, waits for them, and re-layouts  7.88 us

profile of v1, /device:TPU:39, one launch (start us, length us, event | category | flops | bytes accessed | tf_op | source)
XLA Modules:
  0.0 73.1 jit_solution(2103872772745530882)
XLA Ops:
  0.6 0.0 copy-start.4
  0.6 0.6 copy-done.4
  1.3 0.0 copy-start
  1.3 1.1 %copy-done = bf16[768,512]{1,0:T(8,128)(2,1)S(1)} copy-done((bf16[768,512]{1,0:T(8,128)(2,1)S(1)}, bf16[768,512]{1,0:T(8,128)(2,1)}, u32[]{:S(2)}) %copy-start) | copy-done | bytes 786456
  2.4 0.0 copy-start.1
  2.4 1.1 %copy-done.1 = bf16[768,512]{1,0:T(8,128)(2,1)S(1)} copy-done((bf16[768,512]{1,0:T(8,128)(2,1)S(1)}, bf16[768,512]{1,0:T(8,128)(2,1)}, u32[]{:S(2)}) %copy-start.1) | copy-done | bytes 786456
  3.6 0.0 copy-start.2
  3.6 0.9 %copy-done.2 = bf16[768,128]{1,0:T(8,128)(2,1)S(1)} copy-done((bf16[768,128]{1,0:T(8,128)(2,1)S(1)}, bf16[768,128]{1,0:T(8,128)(2,1)}, u32[]{:S(2)}) %copy-start.2) | copy-done | bytes 196632
  4.5 0.0 copy-start.3
  4.5 0.9 %copy-done.3 = bf16[768,128]{1,0:T(8,128)(2,1)S(1)} copy-done((bf16[768,128]{1,0:T(8,128)(2,1)S(1)}, bf16[768,128]{1,0:T(8,128)(2,1)}, u32[]{:S(2)}) %copy-start.3) | copy-done | bytes 196632
  5.4 64.6 %shard_map.84 = (bf16[768,512]{1,0:T(8,128)(2,1)S(1)}, bf16[768,512]{1,0:T(8,128)(2,1)S(1)}, bf16[768,128]{1,0:T(8,128)(2,1)S(1)}, bf16[768,128]{1,0:T(8,128)(2,1)S(1)}) custom-call(bf16[768,512]{1,0:T(8,128)(2,1)S(1)} %copy-done, bf16[768,128]{1,0:T(8,128)(2,1)S(1)} %copy-done.2, bf16[768,128]{1,0:T(8,128)(2,1)S(1)} %copy-done.3, ...), custom_call_target="tpu_custom_call" | custom-call | flops 4300000256 | bytes 4000000 | tf_op jit(solution)/shard_map/pallas_call | solution.py:339
  70.0 0.9 %copy.13 = bf16[768,512]{1,0:T(8,128)(2,1)} copy(bf16[768,512]{1,0:T(8,128)(2,1)S(1)} %get-tuple-element.8) | data formatting | bytes 1572864
  70.9 0.9 %copy.14 = bf16[768,512]{1,0:T(8,128)(2,1)} copy(bf16[768,512]{1,0:T(8,128)(2,1)S(1)} %get-tuple-element.9) | data formatting | bytes 1572864
  71.8 0.7 copy.15
  72.5 0.7 copy.16
Async XLA Ops:
  0.6 0.7 copy-start.4
  1.3 1.1 %copy-start = (bf16[768,512]{1,0:T(8,128)(2,1)S(1)}, bf16[768,512]{1,0:T(8,128)(2,1)}, u32[]{:S(2)}) copy-start(bf16[768,512]{1,0:T(8,128)(2,1)} %q_ref.1) | copy-start | bytes 2359300
  2.4 1.1 %copy-start.1 = (bf16[768,512]{1,0:T(8,128)(2,1)S(1)}, bf16[768,512]{1,0:T(8,128)(2,1)}, u32[]{:S(2)}) copy-start(bf16[768,512]{1,0:T(8,128)(2,1)} %do_ref.1) | copy-start | bytes 2359300
  3.6 0.9 %copy-start.2 = (bf16[768,128]{1,0:T(8,128)(2,1)S(1)}, bf16[768,128]{1,0:T(8,128)(2,1)}, u32[]{:S(2)}) copy-start(bf16[768,128]{1,0:T(8,128)(2,1)} %k_ref.1) | copy-start | bytes 589828
  4.5 0.9 %copy-start.3 = (bf16[768,128]{1,0:T(8,128)(2,1)S(1)}, bf16[768,128]{1,0:T(8,128)(2,1)}, u32[]{:S(2)}) copy-start(bf16[768,128]{1,0:T(8,128)(2,1)} %v_ref.1) | copy-start | bytes 589828

commit v2 on v1

--- a/solution.py
+++ b/solution.py
@@ -18,9 +18,8 @@
 SCALE = 1.0 / math.sqrt(HD)
 SCALE2 = SCALE * math.log2(math.e)
 MESH = pl.DeviceIdType.MESH
-NT = (((1,), (1,)), ((), ()))
-TN = (((0,), (0,)), ((), ()))
-AK, AV, BK, BV, CK, CV, FK, FV, RK, RV, GA, GB, GC, GF, GR, COPIES = range(16)
+NN = (((1,), (0,)), ((), ()))
+AK, AV, BK, BV, CK, CV, FK, FV, RK, RV, GA, GB, HB, GC, GF, GR, HR, COPIES = range(18)
 
 
 def dot(a, b, dims):
@@ -28,9 +27,10 @@
 
 
 def kernel(
-    q_ref, k_ref, v_ref, do_ref, len_ref,
-    att_ref, dq_ref, dk_ref, dv_ref,
-    kbuf, vbuf, first, acck, accv, gout, gin, gfold, relay, grelay, send, recv, fwd,
+    q_hbm, k_hbm, v_hbm, do_hbm, len_ref,
+    att_hbm, dq_hbm, dk_hbm, dv_hbm,
+    q_ref, do_ref, att_ref, dq_ref, dk_ref, dv_ref, kbuf, vbuf, first, acck, accv,
+    gout, gin, gfold, relay, grelay, send, recv, fwd, load, save,
 ):
     d = lax.axis_index("ctx")
     c, k = d // 2, lax.rem(d, 2)
@@ -68,10 +68,18 @@
     greet(cross_u, u2, k)
     greet(cross_w, w2, k)
 
+    loads = [
+        pltpu.make_async_copy(q_hbm, q_ref, load.at[0]),
+        pltpu.make_async_copy(do_hbm, do_ref, load.at[1]),
+    ]
     for slot in range(2):
-        rows = slice(slot * CH, (slot + 1) * CH)
-        kbuf[slot, OWN:] = k_ref[rows]
-        vbuf[slot, OWN:] = v_ref[rows]
+        rows, place = pl.ds(slot * CH, CH), pl.ds(OWN, CH)
+        loads += [
+            pltpu.make_async_copy(k_hbm.at[rows], kbuf.at[slot, place], load.at[2 + 2 * slot]),
+            pltpu.make_async_copy(v_hbm.at[rows], vbuf.at[slot, place], load.at[3 + 2 * slot]),
+        ]
+    for copy in loads:
+        copy.start()
 
     @pl.when((c == 0) & (k == 0))
     def _():
@@ -118,20 +126,20 @@
     near, far = pl.ds(CH, CH), pl.ds(0, CH)
     mine, theirs = pl.ds(k * CH, CH), pl.ds(other * CH, CH)
     send_a = [
-        remote(k_ref.at[theirs], kbuf.at[other, near], AK, u, other),
-        remote(v_ref.at[theirs], vbuf.at[other, near], AV, u, other),
+        remote(k_hbm.at[theirs], kbuf.at[other, near], AK, u, other),
+        remote(v_hbm.at[theirs], vbuf.at[other, near], AV, u, other),
     ]
     send_b = [
-        remote(k_ref.at[mine], kbuf.at[k, far], BK, w, k),
-        remote(v_ref.at[mine], vbuf.at[k, far], BV, w, k),
+        remote(k_hbm.at[mine], kbuf.at[k, far], BK, w, k),
+        remote(v_hbm.at[mine], vbuf.at[k, far], BV, w, k),
     ]
     send_r = [
-        remote(k_ref.at[mine], relay.at[0], RK, u, k),
-        remote(v_ref.at[mine], relay.at[1], RV, u, k),
+        remote(k_hbm.at[mine], relay.at[0], RK, u, k),
+        remote(v_hbm.at[mine], relay.at[1], RV, u, k),
     ]
     send_c = [
-        remote(k_ref.at[mine], kbuf.at[k, near], CK, c, other),
-        remote(v_ref.at[mine], vbuf.at[k, near], CV, c, other),
+        remote(k_hbm.at[mine], kbuf.at[k, near], CK, c, other),
+        remote(v_hbm.at[mine], vbuf.at[k, near], CV, c, other),
     ]
     send_f = [
         remote(kbuf.at[k, near], kbuf.at[k, far], FK, c, other),
@@ -142,12 +150,18 @@
         remote(relay.at[1], vbuf.at[k, far], BV, w2, k, fwd.at[1]),
     ]
     send_ga = remote(gout.at[k, 1], gin.at[0], GA, u, other)
-    send_gb = remote(gout.at[k, 0], gin.at[1], GB, u, k)
-    send_gfold = remote(gout.at[k, 0], gin.at[1], GB, c, other)
-    send_gr = remote(gout.at[k, 0], grelay, GR, w, k)
+    halves = [pl.ds(0, CH), pl.ds(CH, CH)]
+    send_gb = [remote(gout.at[k, 0, h], gin.at[1, h], GB + i, u, k) for i, h in enumerate(halves)]
+    send_gfold = [
+        remote(gout.at[k, 0, h], gin.at[1, h], GB + i, c, other) for i, h in enumerate(halves)
+    ]
+    send_gr = [remote(gout.at[k, 0, h], grelay.at[h], GR + i, w, k) for i, h in enumerate(halves)]
     send_gc = remote(gout.at[other, 1], gin.at[2], GC, c, other)
     send_gf = remote(gout.at[other, 0], gfold, GF, c, other)
-    pass_g = remote(grelay, gin.at[1], GB, u2, k, fwd.at[2])
+    pass_g = [
+        remote(grelay.at[h], gin.at[1, h], GB + i, u2, k, fwd.at[2 + i])
+        for i, h in enumerate(halves)
+    ]
 
     def start(when, copies):
         @pl.when(when)
@@ -173,20 +187,24 @@
     def prepare(slot):
         @pl.when(slot == k)
         def _():
-            @pl.when(has_u)
-            def _():
-                landed(kbuf.at[k, near], AK)
-                landed(vbuf.at[k, near], AV)
-
             @pl.when(fold)
             def _():
-                kbuf[1, CH:OWN] = k_ref[:CH]
-                vbuf[1, CH:OWN] = v_ref[:CH]
+                kbuf[1, CH:OWN] = kbuf[0, OWN:]
+                vbuf[1, CH:OWN] = vbuf[0, OWN:]
                 kbuf[1, :CH] = kbuf[0, CH:OWN]
                 vbuf[1, :CH] = vbuf[0, CH:OWN]
 
-            for copy in send_f:
-                copy.start()
+            @pl.when(has_u)
+            def _():
+                landed(kbuf.at[k, near], AK)
+
+            send_f[0].start()
+
+            @pl.when(has_u)
+            def _():
+                landed(vbuf.at[k, near], AV)
+
+            send_f[1].start()
 
             @pl.when(has_u)
             def _():
@@ -209,40 +227,33 @@
             key_line = lax.broadcasted_iota(jnp.int32, (WIN, SUB), 0)
             query_lane = lax.broadcasted_iota(jnp.int32, (WIN, SUB), 1)
             allowed = (key_line - OWN <= query_lane) & (key_line >= first[slot, sub][:1])
-            bias = jnp.where(allowed, 0.0, MASKED)
-            bias = jnp.concatenate([bias, bias], axis=1)
-            grad_k = grad_v = None
-            for pair in range(QH // 2):
-                heads = [slice(h * HD, (h + 1) * HD) for h in (2 * pair, 2 * pair + 1)]
-                query = jnp.concatenate([q_ref[rows, h] for h in heads], axis=0)
-                dout = jnp.concatenate([do_ref[rows, h] for h in heads], axis=0)
-                scores = dot(keys, query, NT) * SCALE2 + bias
-                top = jnp.max(scores, axis=0, keepdims=True)
-                raised = jnp.exp2(scores - top)
-                total = jnp.sum(raised, axis=0, keepdims=True)
-                weights = (raised * (1.0 / total)).astype(jnp.bfloat16)
-                attended = dot(weights, values, TN).astype(jnp.bfloat16)
-                product = dout.astype(jnp.float32) * attended.astype(jnp.float32)
-                delta = lax.dot_general(
-                    jnp.ones((8, HD), jnp.float32), product, NT,
-                    precision=lax.Precision.HIGHEST, preferred_element_type=jnp.float32,
-                )[:1]
-                dprob = dot(values, dout, NT)
-                dscore = (weights.astype(jnp.float32) * (dprob - delta)).astype(jnp.bfloat16)
-                grad_q = (dot(dscore, keys, TN) * SCALE).astype(jnp.bfloat16)
-                for half in range(2):
-                    part = slice(half * SUB, (half + 1) * SUB)
-                    att_ref[rows, heads[half]] = attended[part]
-                    dq_ref[rows, heads[half]] = grad_q[part]
-                new_k = dot(dscore, query, (((1,), (0,)), ((), ())))
-                new_v = dot(weights, dout, (((1,), (0,)), ((), ())))
-                grad_k = new_k if grad_k is None else grad_k + new_k
-                grad_v = new_v if grad_v is None else grad_v + new_v
-            acck[slot, window] = acck[slot, window] + grad_k
-            accv[slot, window] = accv[slot, window] + grad_v
+            bias = jnp.concatenate([jnp.where(allowed, 0.0, MASKED)] * QH, axis=1)
+            heads = [slice(h * HD, (h + 1) * HD) for h in range(QH)]
+            query = jnp.concatenate([q_ref[rows, h] for h in heads], axis=0)
+            dout = jnp.concatenate([do_ref[rows, h] for h in heads], axis=0)
+            dout_t = dout.T
+            scores = dot(keys, query.T, NN) * SCALE2 + bias
+            top = jnp.max(scores, axis=0, keepdims=True)
+            raised = jnp.exp2(scores - top)
+            total = jnp.sum(raised, axis=0, keepdims=True)
+            weights = (raised * (1.0 / total)).astype(jnp.bfloat16)
+            attended = dot(values.T, weights, NN).astype(jnp.bfloat16)
+            delta = jnp.sum(
+                dout_t.astype(jnp.float32) * attended.astype(jnp.float32), axis=0, keepdims=True
+            )
+            dprob = dot(values, dout_t, NN)
+            dscore = (weights.astype(jnp.float32) * (dprob - delta)).astype(jnp.bfloat16)
+            grad_q = (dot(keys.T, dscore, NN) * SCALE).astype(jnp.bfloat16).T
+            attended = attended.T
+            for h in range(QH):
+                part = slice(h * SUB, (h + 1) * SUB)
+                att_ref[rows, heads[h]] = attended[part]
+                dq_ref[rows, heads[h]] = grad_q[part]
+            acck[slot, window] = acck[slot, window] + dot(dscore, query, NN)
+            accv[slot, window] = accv[slot, window] + dot(weights, dout, NN)
             return carry
 
-        lax.fori_loop(0, 3, tile, 0)
+        lax.fori_loop(0, 3, tile, 0, unroll=3)
 
     def give(slot):
         @pl.when(slot == other)
@@ -258,9 +269,9 @@
         def _():
             gout[k, 0, :CH] = acck[k, :CH].astype(jnp.bfloat16)
             gout[k, 0, CH:] = accv[k, :CH].astype(jnp.bfloat16)
-            start(near_u, [send_gb])
-            start(cross_u, [send_gr])
-            start(fold, [send_gfold])
+            start(near_u, send_gb)
+            start(cross_u, send_gr)
+            start(fold, send_gfold)
             send_gf.wait_recv()
             sum_k = acck[k, CH:OWN] + gfold[:CH].astype(jnp.float32)
             sum_v = accv[k, CH:OWN] + gfold[CH:].astype(jnp.float32)
@@ -275,6 +286,16 @@
             def _():
                 acck[0, OWN:] = acck[0, OWN:] + sum_k
                 accv[0, OWN:] = accv[0, OWN:] + sum_v
+
+    for copy in loads:
+        copy.wait()
+
+    def saves(slot):
+        rows = pl.ds(slot * CH, CH)
+        return [
+            pltpu.make_async_copy(att_ref.at[rows], att_hbm.at[rows], save.at[2 * slot]),
+            pltpu.make_async_copy(dq_ref.at[rows], dq_hbm.at[rows], save.at[2 * slot + 1]),
+        ]
 
     early = (y < 2).astype(jnp.int32)
 
@@ -283,14 +304,17 @@
         prepare(slot)
         attend(slot)
         give(slot)
+        for copy in saves(slot):
+            copy.start()
         return carry
 
     lax.fori_loop(0, 2, turn, 0)
 
     @pl.when(relay_g)
     def _():
-        send_gr.wait_recv()
-        pass_g.start()
+        for come, go in zip(send_gr, pass_g):
+            come.wait_recv()
+            go.start()
 
     def add(slot, which):
         acck[slot, OWN:] = acck[slot, OWN:] + gin[which, :CH].astype(jnp.float32)
@@ -306,13 +330,21 @@
 
     @pl.when(has_w | folded)
     def _():
-        send_gb.wait_recv()
+        for copy in send_gb:
+            copy.wait_recv()
         add(k, 1)
 
     for slot in range(2):
         rows = slice(slot * CH, (slot + 1) * CH)
         dk_ref[rows] = (acck[slot, OWN:] * SCALE).astype(jnp.bfloat16)
         dv_ref[rows] = accv[slot, OWN:].astype(jnp.bfloat16)
+
+    last = [
+        pltpu.make_async_copy(dk_ref, dk_hbm, save.at[4]),
+        pltpu.make_async_copy(dv_ref, dv_hbm, save.at[5]),
+    ]
+    for copy in last:
+        copy.start()
 
     def sent(when, copies):
         @pl.when(when)
@@ -326,27 +358,52 @@
     sent(near_w, send_b)
     sent(cross_w, send_r)
     sent(relay_kv, pass_on)
-    sent(near_u, [send_gb])
-    sent(cross_u, [send_gr])
-    sent(fold, [send_gfold])
-    sent(relay_g, [pass_g])
+    sent(near_u, send_gb)
+    sent(cross_u, send_gr)
+    sent(fold, send_gfold)
+    sent(relay_g, pass_g)
+    for copy in saves(0) + saves(1) + last:
+        copy.wait()
+
+
+def write(*refs):
+    sources, outs, held, came, done = refs[:4], refs[4:8], refs[8:12], refs[12], refs[13]
+    loads = [
+        pltpu.make_async_copy(src, buf, came.at[i])
+        for i, (src, buf) in enumerate(zip(sources, held))
+    ]
+    copies = [
+        pltpu.make_async_copy(buf, out, done.at[i])
+        for i, (buf, out) in enumerate(zip(held, outs))
+    ]
+    for copy in loads:
+        copy.start()
+    for load, copy in zip(loads, copies):
+        load.wait()
+        copy.start()
+    for copy in copies:
+        copy.wait()
 
 
 def body(query, key, value, d_out, doc_lengths):
     rows, features = query.shape
     vmem = pl.BlockSpec(memory_space=pltpu.VMEM)
+    hbm = pl.BlockSpec(memory_space=pltpu.HBM)
     bf16, f32 = jnp.bfloat16, jnp.float32
-    return pl.pallas_call(
+    shapes = [
+        jax.ShapeDtypeStruct((rows, features), bf16),
+        jax.ShapeDtypeStruct((rows, features), bf16),
+        jax.ShapeDtypeStruct((rows, HD), bf16),
+        jax.ShapeDtypeStruct((rows, HD), bf16),
+    ]
+    made = pl.pallas_call(
         kernel,
-        out_shape=[
-            jax.ShapeDtypeStruct((rows, features), bf16),
-            jax.ShapeDtypeStruct((rows, features), bf16),
-            jax.ShapeDtypeStruct((rows, HD), bf16),
-            jax.ShapeDtypeStruct((rows, HD), bf16),
-        ],
-        in_specs=[vmem] * 5,
-        out_specs=[vmem] * 4,
+        out_shape=shapes,
+        in_specs=[hbm] * 4 + [vmem],
+        out_specs=[hbm] * 4,
         scratch_shapes=[
+            *[pltpu.VMEM((rows, features), bf16)] * 4,
+            *[pltpu.VMEM((rows, HD), bf16)] * 2,
             pltpu.VMEM((2, 3 * CH, HD), bf16),
             pltpu.VMEM((2, 3 * CH, HD), bf16),
             pltpu.VMEM((2, 3, 8, HD), jnp.int32),
@@ -359,15 +416,30 @@
             pltpu.VMEM((2 * CH, HD), bf16),
             pltpu.SemaphoreType.DMA((COPIES,)),
             pltpu.SemaphoreType.DMA((COPIES,)),
-            pltpu.SemaphoreType.DMA((3,)),
+            pltpu.SemaphoreType.DMA((4,)),
+            pltpu.SemaphoreType.DMA((6,)),
+            pltpu.SemaphoreType.DMA((6,)),
         ],
         compiler_params=pltpu.CompilerParams(
-            collective_id=0, has_side_effects=True, vmem_limit_bytes=48 * 2**20
+            collective_id=0, has_side_effects=True, vmem_limit_bytes=60_000_000
         ),
         cost_estimate=pl.CostEstimate(
             flops=4_300_000_000, bytes_accessed=4_000_000, transcendentals=2_800_000
         ),
     )(query, key, value, d_out, doc_lengths.reshape(1, -1))
+    return pl.pallas_call(
+        write,
+        out_shape=shapes,
+        in_specs=[hbm] * 4,
+        out_specs=[hbm] * 4,
+        scratch_shapes=[
+            *[pltpu.VMEM(shape.shape, bf16) for shape in shapes],
+            pltpu.SemaphoreType.DMA((4,)),
+            pltpu.SemaphoreType.DMA((4,)),
+        ],
+        compiler_params=pltpu.CompilerParams(vmem_limit_bytes=60_000_000),
+        cost_estimate=pl.CostEstimate(flops=0, bytes_accessed=4_000_000, transcendentals=0),
+    )(*made)
 
 
 def solution(mesh):

time: 73.4 us -> 62.3 us (0.85)
  local copies, waits for them, and re-layouts: 7.88 us -> 0 us
  Pallas kernels: 64.6 us -> 61.5 us
    unnamed x14 -> x0, local copies, waits for them, and re-layouts: 7.88 us -> none
    pallas_call x1 -> x2, Pallas kernels: 64.6 us -> 61.5 us  [the longest x1 59 us: body(): pl.pallas_call(kernel, out_shape=shapes, in_specs=[hbm] * 4 + [vmem], out...]
where the time goes in v2:
time: 62.3 us; the launch traced here: 62.1 us
  Pallas kernels  61.5 us (99%)
  between operations  0.64 us (1%)
    pallas_call x1, Pallas kernels, body(): pl.pallas_call(kernel, out_shape=shapes, in_specs=[hbm] * 4 + [vmem], out...  59 us
    pallas_call x1, Pallas kernels, body(): pl.pallas_call(write, out_shape=shapes, in_specs=[hbm] * 4, out_specs=[hb...  2.46 us

profile of v2, /device:TPU:39, one launch (start us, length us, event | category | flops | bytes accessed | tf_op | source)
XLA Modules:
  0.0 62.1 jit_solution(18308730459197883139)
XLA Ops:
  0.6 59.0 %shard_map.84 = (bf16[768,512]{1,0:T(8,128)(2,1)}, bf16[768,512]{1,0:T(8,128)(2,1)}, bf16[768,128]{1,0:T(8,128)(2,1)}, bf16[768,128]{1,0:T(8,128)(2,1)}) custom-call(bf16[768,512]{1,0:T(8,128)(2,1)} %q_hbm.1, bf16[768,128]{1,0:T(8,128)(2,1)} %k_hbm.1, bf16[768,128]{1,0:T(8,128)(2,1)} %v_hbm.1, bf16[768,512]{1,0:T(8,128)(2,1)} %do_hbm.1, s32[1,128]{1,0:T(1,128)} %bitcast.1), custom_call_target="tpu_custom_call" | custom-call | flops 4300000256 | bytes 4000000 | tf_op jit(solution)/shard_map/pallas_call | solution.py:399
  59.7 2.5 %shard_map.85 = (bf16[768,512]{1,0:T(8,128)(2,1)}, bf16[768,512]{1,0:T(8,128)(2,1)}, bf16[768,128]{1,0:T(8,128)(2,1)}, bf16[768,128]{1,0:T(8,128)(2,1)}) custom-call(bf16[768,512]{1,0:T(8,128)(2,1)} %get-tuple-element.8.refs_0_, bf16[768,512]{1,0:T(8,128)(2,1)} %get-tuple-element.9.refs_1_, bf16[768,128]{1,0:T(8,128)(2,1)} %get-tuple-element.10.refs_2_, ...), custom_call_target="tpu_custom_call" | custom-call | bytes 4000000 | tf_op jit(solution)/shard_map/pallas_call | solution.py:430

commit v3 on v2

--- a/solution.py
+++ b/solution.py
@@ -17,6 +17,7 @@
 MASKED = -1e30
 SCALE = 1.0 / math.sqrt(HD)
 SCALE2 = SCALE * math.log2(math.e)
+LATER = (3, 5, 8)
 MESH = pl.DeviceIdType.MESH
 NN = (((1,), (0,)), ((), ()))
 AK, AV, BK, BV, CK, CV, FK, FV, RK, RV, GA, GB, HB, GC, GF, GR, HR, COPIES = range(18)
@@ -30,7 +31,7 @@
     q_hbm, k_hbm, v_hbm, do_hbm, len_ref,
     att_hbm, dq_hbm, dk_hbm, dv_hbm,
     q_ref, do_ref, att_ref, dq_ref, dk_ref, dv_ref, kbuf, vbuf, first, acck, accv,
-    gout, gin, gfold, relay, grelay, send, recv, fwd, load, save,
+    wbuf, delta, turned, accq, gout, gin, gfold, relay, grelay, send, recv, fwd, load, save,
 ):
     d = lax.axis_index("ctx")
     c, k = d // 2, lax.rem(d, 2)
@@ -86,9 +87,6 @@
         kbuf[0, :OWN] = jnp.zeros((OWN, HD), jnp.bfloat16)
         vbuf[0, :OWN] = jnp.zeros((OWN, HD), jnp.bfloat16)
 
-    acck[...] = jnp.zeros_like(acck)
-    accv[...] = jnp.zeros_like(accv)
-
     lens = jnp.broadcast_to(len_ref[...], (HD, HD))
     line = lax.broadcasted_iota(jnp.int32, (HD, HD), 0)
     lane = lax.broadcasted_iota(jnp.int32, (HD, HD), 1)
@@ -169,109 +167,136 @@
             for copy in copies:
                 copy.start()
 
-    start(has_u, send_a)
+    z_low = lax.axis_index("dp")
+    group = sum((z_low >= bound).astype(jnp.int32) for bound in LATER)
+
+    def send_far(when):
+        start(cross_u & when, send_a)
+
+        @pl.when(relay_kv & when)
+        def _():
+            for come, go in zip(send_r, pass_on):
+                come.wait_recv()
+                go.start()
+
+    start(near_u, send_a)
     start(cross_w, send_r)
     start(near_w, send_b)
     for copy in send_c:
         copy.start()
-
-    @pl.when(relay_kv)
-    def _():
-        for come, go in zip(send_r, pass_on):
-            come.wait_recv()
-            go.start()
+    send_far(group == 0)
 
     def landed(dst, which):
         remote(dst, dst, which, c, other).wait_recv()
 
-    def prepare(slot):
+    def arrive(slot, buf, copy_f, which):
+        of_a, of_b, of_c, of_f = which
+
         @pl.when(slot == k)
         def _():
             @pl.when(fold)
             def _():
-                kbuf[1, CH:OWN] = kbuf[0, OWN:]
-                vbuf[1, CH:OWN] = vbuf[0, OWN:]
-                kbuf[1, :CH] = kbuf[0, CH:OWN]
-                vbuf[1, :CH] = vbuf[0, CH:OWN]
+                buf[1, CH:OWN] = buf[0, OWN:]
+                buf[1, :CH] = buf[0, CH:OWN]
 
             @pl.when(has_u)
             def _():
-                landed(kbuf.at[k, near], AK)
-
-            send_f[0].start()
+                landed(buf.at[k, near], of_a)
+
+            copy_f.start()
 
             @pl.when(has_u)
             def _():
-                landed(vbuf.at[k, near], AV)
-
-            send_f[1].start()
-
-            @pl.when(has_u)
-            def _():
-                landed(kbuf.at[k, far], BK)
-                landed(vbuf.at[k, far], BV)
+                landed(buf.at[k, far], of_b)
 
         @pl.when(slot == other)
         def _():
-            landed(kbuf.at[other, near], CK)
-            landed(vbuf.at[other, near], CV)
-            landed(kbuf.at[other, far], FK)
-            landed(vbuf.at[other, far], FV)
-
-    def attend(slot):
-        def tile(sub, carry):
-            rows = pl.ds(pl.multiple_of(slot * CH + sub * SUB, SUB), SUB)
-            window = pl.ds(pl.multiple_of(sub * SUB, SUB), WIN)
-            keys = kbuf[slot, window]
-            values = vbuf[slot, window]
+            landed(buf.at[other, near], of_c)
+            landed(buf.at[other, far], of_f)
+
+    def head_rows(ref, slot, sub):
+        rows = pl.ds(pl.multiple_of(slot * CH + sub * SUB, SUB), SUB)
+        return jnp.concatenate([ref[rows, h * HD : (h + 1) * HD] for h in range(QH)], axis=0)
+
+    def store_heads(ref, slot, sub, value):
+        rows = pl.ds(pl.multiple_of(slot * CH + sub * SUB, SUB), SUB)
+        for h in range(QH):
+            ref[rows, h * HD : (h + 1) * HD] = value[h * SUB : (h + 1) * SUB]
+
+    def weigh(slot):
+        for sub in range(3):
+            keys = kbuf[slot, sub * SUB : sub * SUB + WIN]
             key_line = lax.broadcasted_iota(jnp.int32, (WIN, SUB), 0)
             query_lane = lax.broadcasted_iota(jnp.int32, (WIN, SUB), 1)
             allowed = (key_line - OWN <= query_lane) & (key_line >= first[slot, sub][:1])
             bias = jnp.concatenate([jnp.where(allowed, 0.0, MASKED)] * QH, axis=1)
-            heads = [slice(h * HD, (h + 1) * HD) for h in range(QH)]
-            query = jnp.concatenate([q_ref[rows, h] for h in heads], axis=0)
-            dout = jnp.concatenate([do_ref[rows, h] for h in heads], axis=0)
-            dout_t = dout.T
-            scores = dot(keys, query.T, NN) * SCALE2 + bias
+            scores = dot(keys, head_rows(q_ref, slot, sub).T, NN) * SCALE2 + bias
             top = jnp.max(scores, axis=0, keepdims=True)
             raised = jnp.exp2(scores - top)
             total = jnp.sum(raised, axis=0, keepdims=True)
-            weights = (raised * (1.0 / total)).astype(jnp.bfloat16)
-            attended = dot(values.T, weights, NN).astype(jnp.bfloat16)
-            delta = jnp.sum(
-                dout_t.astype(jnp.float32) * attended.astype(jnp.float32), axis=0, keepdims=True
-            )
-            dprob = dot(values, dout_t, NN)
-            dscore = (weights.astype(jnp.float32) * (dprob - delta)).astype(jnp.bfloat16)
-            grad_q = (dot(keys.T, dscore, NN) * SCALE).astype(jnp.bfloat16).T
-            attended = attended.T
-            for h in range(QH):
-                part = slice(h * SUB, (h + 1) * SUB)
-                att_ref[rows, heads[h]] = attended[part]
-                dq_ref[rows, heads[h]] = grad_q[part]
-            acck[slot, window] = acck[slot, window] + dot(dscore, query, NN)
-            accv[slot, window] = accv[slot, window] + dot(weights, dout, NN)
-            return carry
-
-        lax.fori_loop(0, 3, tile, 0, unroll=3)
-
-    def give(slot):
+            wbuf[sub] = (raised * (1.0 / total)).astype(jnp.bfloat16)
+
+    def attend(slot):
+        for sub in range(3):
+            values = vbuf[slot, sub * SUB : sub * SUB + WIN]
+            attended = dot(values.T, wbuf[sub], NN).astype(jnp.bfloat16)
+            dout_t = head_rows(do_ref, slot, sub).T
+            product = dout_t.astype(jnp.float32) * attended.astype(jnp.float32)
+            delta[sub] = jnp.broadcast_to(jnp.sum(product, axis=0, keepdims=True), (8, QH * SUB))
+            turned[sub] = dout_t
+            store_heads(att_ref, slot, sub, attended.T)
+
+    def backward(slot, place, order):
+        for sub in order:
+            low = max(place * CH, sub * SUB)
+            high = min(place * CH + CH, sub * SUB + WIN)
+            keys = kbuf[slot, low:high]
+            values = vbuf[slot, low:high]
+            weights = wbuf[sub, low - sub * SUB : high - sub * SUB]
+            dprob = dot(values, turned[sub], NN)
+            dscore = (weights.astype(jnp.float32) * (dprob - delta[sub][:1])).astype(jnp.bfloat16)
+            grad_k = dot(dscore, head_rows(q_ref, slot, sub), NN)
+            grad_v = dot(weights, head_rows(do_ref, slot, sub), NN)
+            grad_q = dot(keys.T, dscore, NN)
+            if sub == order[0]:
+                acck[slot, low:high] = grad_k
+                accv[slot, low:high] = grad_v
+            else:
+                acck[slot, low:high] = acck[slot, low:high] + grad_k
+                accv[slot, low:high] = accv[slot, low:high] + grad_v
+            if place == 0:
+                accq[sub] = grad_q
+            elif place == 1:
+                accq[sub] = accq[sub] + grad_q
+            else:
+                grad_q = ((accq[sub] + grad_q) * SCALE).astype(jnp.bfloat16)
+                store_heads(dq_ref, slot, sub, grad_q.T)
+
+    def pack(slot, place):
+        rows = slice(place * CH, (place + 1) * CH)
+        gout[slot, place, :CH] = acck[slot, rows].astype(jnp.bfloat16)
+        gout[slot, place, CH:] = accv[slot, rows].astype(jnp.bfloat16)
+
+    def give_far(slot):
+        pack(slot, 0)
+
         @pl.when(slot == other)
         def _():
-            for place in range(2):
-                rows = slice(place * CH, (place + 1) * CH)
-                gout[other, place, :CH] = acck[other, rows].astype(jnp.bfloat16)
-                gout[other, place, CH:] = accv[other, rows].astype(jnp.bfloat16)
             send_gf.start()
+
+        start((slot == k) & near_u, send_gb)
+        start((slot == k) & cross_u, send_gr)
+        start((slot == k) & fold, send_gfold)
+
+    def give_near(slot):
+        @pl.when(slot == other)
+        def _():
+            pack(other, 1)
             send_gc.start()
 
+    def give_sum(slot):
         @pl.when(slot == k)
         def _():
-            gout[k, 0, :CH] = acck[k, :CH].astype(jnp.bfloat16)
-            gout[k, 0, CH:] = accv[k, :CH].astype(jnp.bfloat16)
-            start(near_u, send_gb)
-            start(cross_u, send_gr)
-            start(fold, send_gfold)
             send_gf.wait_recv()
             sum_k = acck[k, CH:OWN] + gfold[:CH].astype(jnp.float32)
             sum_v = accv[k, CH:OWN] + gfold[CH:].astype(jnp.float32)
@@ -301,9 +326,19 @@
 
     def turn(index, carry):
         slot = early + index - 2 * early * index
-        prepare(slot)
+        arrive(slot, kbuf, send_f[0], (AK, BK, CK, FK))
+        send_far((index == 0) & (group == 1))
+        weigh(slot)
+        send_far((index == 0) & (group == 2))
+        arrive(slot, vbuf, send_f[1], (AV, BV, CV, FV))
         attend(slot)
-        give(slot)
+        send_far((index == 0) & (group == 3))
+        backward(slot, 0, (0, 1, 2))
+        give_far(slot)
+        backward(slot, 1, (0, 1, 2))
+        give_near(slot)
+        backward(slot, 2, (2, 1, 0))
+        give_sum(slot)
         for copy in saves(slot):
             copy.start()
         return carry
@@ -409,6 +444,10 @@
             pltpu.VMEM((2, 3, 8, HD), jnp.int32),
             pltpu.VMEM((2, 3 * CH, HD), f32),
             pltpu.VMEM((2, 3 * CH, HD), f32),
+            pltpu.VMEM((3, WIN, QH * SUB), bf16),
+            pltpu.VMEM((3, 8, QH * SUB), f32),
+            pltpu.VMEM((3, HD, QH * SUB), bf16),
+            pltpu.VMEM((3, HD, QH * SUB), f32),
             pltpu.VMEM((2, 2, 2 * CH, HD), bf16),
             pltpu.VMEM((3, 2 * CH, HD), bf16),
             pltpu.VMEM((2 * CH, HD), bf16),

time: 62.3 us -> 56.2 us (0.902)
  the two profiles are of different devices: /device:TPU:39 before, /device:TPU:199 now
where the time goes in v3:
time: 56.2 us; the launch traced here: 56 us
  Pallas kernels  55.4 us (99%)
  between operations  0.64 us (1%)
    pallas_call x1, Pallas kernels, body(): pl.pallas_call(kernel, out_shape=shapes, in_specs=[hbm] * 4 + [vmem], out...  52.9 us
    pallas_call x1, Pallas kernels, body(): pl.pallas_call(write, out_shape=shapes, in_specs=[hbm] * 4, out_specs=[hb...  2.46 us

profile of v3, /device:TPU:199, one launch (start us, length us, event | category | flops | bytes accessed | tf_op | source)
XLA Modules:
  0.0 56.0 jit_solution(4437044635193937042)
XLA Ops:
  0.6 52.9 %shard_map.84 = (bf16[768,512]{1,0:T(8,128)(2,1)}, bf16[768,512]{1,0:T(8,128)(2,1)}, bf16[768,128]{1,0:T(8,128)(2,1)}, bf16[768,128]{1,0:T(8,128)(2,1)}) custom-call(bf16[768,512]{1,0:T(8,128)(2,1)} %q_hbm.1, bf16[768,128]{1,0:T(8,128)(2,1)} %k_hbm.1, bf16[768,128]{1,0:T(8,128)(2,1)} %v_hbm.1, bf16[768,512]{1,0:T(8,128)(2,1)} %do_hbm.1, s32[1,128]{1,0:T(1,128)} %bitcast.1), custom_call_target="tpu_custom_call" | custom-call | flops 4300000256 | bytes 4000000 | tf_op jit(solution)/shard_map/pallas_call | solution.py:434
  53.6 2.5 %shard_map.85 = (bf16[768,512]{1,0:T(8,128)(2,1)}, bf16[768,512]{1,0:T(8,128)(2,1)}, bf16[768,128]{1,0:T(8,128)(2,1)}, bf16[768,128]{1,0:T(8,128)(2,1)}) custom-call(bf16[768,512]{1,0:T(8,128)(2,1)} %get-tuple-element.8.refs_0_, bf16[768,512]{1,0:T(8,128)(2,1)} %get-tuple-element.9.refs_1_, bf16[768,128]{1,0:T(8,128)(2,1)} %get-tuple-element.10.refs_2_, ...), custom_call_target="tpu_custom_call" | custom-call | bytes 4000000 | tf_op jit(solution)/shard_map/pallas_call | solution.py:469

commit v4 on v3

--- a/solution.py
+++ b/solution.py
@@ -31,7 +31,7 @@
     q_hbm, k_hbm, v_hbm, do_hbm, len_ref,
     att_hbm, dq_hbm, dk_hbm, dv_hbm,
     q_ref, do_ref, att_ref, dq_ref, dk_ref, dv_ref, kbuf, vbuf, first, acck, accv,
-    wbuf, delta, turned, accq, gout, gin, gfold, relay, grelay, send, recv, fwd, load, save,
+    wbuf, delta, mask, asked, turned, accq, gout, gin, gfold, relay, grelay, send, recv, fwd, load, save,
 ):
     d = lax.axis_index("ctx")
     c, k = d // 2, lax.rem(d, 2)
@@ -223,14 +223,20 @@
         for h in range(QH):
             ref[rows, h * HD : (h + 1) * HD] = value[h * SUB : (h + 1) * SUB]
 
+    def ready(slot):
+        for sub in range(3):
+            asked[sub] = head_rows(q_ref, slot, sub).T
+            turned[sub] = head_rows(do_ref, slot, sub).T
+            key_line = lax.broadcasted_iota(jnp.int32, (WIN, SUB), 0)
+            query_lane = lax.broadcasted_iota(jnp.int32, (WIN, SUB), 1)
+            allowed = (key_line - OWN <= query_lane) & (key_line >= first[slot, sub][:1])
+            mask[sub] = jnp.where(allowed, 0.0, MASKED)
+
     def weigh(slot):
         for sub in range(3):
             keys = kbuf[slot, sub * SUB : sub * SUB + WIN]
-            key_line = lax.broadcasted_iota(jnp.int32, (WIN, SUB), 0)
-            query_lane = lax.broadcasted_iota(jnp.int32, (WIN, SUB), 1)
-            allowed = (key_line - OWN <= query_lane) & (key_line >= first[slot, sub][:1])
-            bias = jnp.concatenate([jnp.where(allowed, 0.0, MASKED)] * QH, axis=1)
-            scores = dot(keys, head_rows(q_ref, slot, sub).T, NN) * SCALE2 + bias
+            bias = jnp.concatenate([mask[sub]] * QH, axis=1)
+            scores = dot(keys, asked[sub], NN) * SCALE2 + bias
             top = jnp.max(scores, axis=0, keepdims=True)
             raised = jnp.exp2(scores - top)
             total = jnp.sum(raised, axis=0, keepdims=True)
@@ -240,10 +246,8 @@
         for sub in range(3):
             values = vbuf[slot, sub * SUB : sub * SUB + WIN]
             attended = dot(values.T, wbuf[sub], NN).astype(jnp.bfloat16)
-            dout_t = head_rows(do_ref, slot, sub).T
-            product = dout_t.astype(jnp.float32) * attended.astype(jnp.float32)
+            product = turned[sub].astype(jnp.float32) * attended.astype(jnp.float32)
             delta[sub] = jnp.broadcast_to(jnp.sum(product, axis=0, keepdims=True), (8, QH * SUB))
-            turned[sub] = dout_t
             store_heads(att_ref, slot, sub, attended.T)
 
     def backward(slot, place, order):
@@ -326,6 +330,7 @@
 
     def turn(index, carry):
         slot = early + index - 2 * early * index
+        ready(slot)
         arrive(slot, kbuf, send_f[0], (AK, BK, CK, FK))
         send_far((index == 0) & (group == 1))
         weigh(slot)
@@ -358,10 +363,26 @@
     send_gc.wait_recv()
     add(k, 2)
 
+    def finish(slot):
+        rows = pl.ds(pl.multiple_of(slot * CH, SUB), CH)
+        dk_ref[rows] = (acck[slot, OWN:] * SCALE).astype(jnp.bfloat16)
+        dv_ref[rows] = accv[slot, OWN:].astype(jnp.bfloat16)
+        for copy in last(slot):
+            copy.start()
+
+    def last(slot):
+        rows = pl.ds(pl.multiple_of(slot * CH, SUB), CH)
+        return [
+            pltpu.make_async_copy(dk_ref.at[rows], dk_hbm.at[rows], save.at[4 + 2 * slot]),
+            pltpu.make_async_copy(dv_ref.at[rows], dv_hbm.at[rows], save.at[5 + 2 * slot]),
+        ]
+
     @pl.when(has_u)
     def _():
         send_ga.wait_recv()
         add(other, 0)
+
+    finish(other)
 
     @pl.when(has_w | folded)
     def _():
@@ -369,17 +390,7 @@
             copy.wait_recv()
         add(k, 1)
 
-    for slot in range(2):
-        rows = slice(slot * CH, (slot + 1) * CH)
-        dk_ref[rows] = (acck[slot, OWN:] * SCALE).astype(jnp.bfloat16)
-        dv_ref[rows] = accv[slot, OWN:].astype(jnp.bfloat16)
-
-    last = [
-        pltpu.make_async_copy(dk_ref, dk_hbm, save.at[4]),
-        pltpu.make_async_copy(dv_ref, dv_hbm, save.at[5]),
-    ]
-    for copy in last:
-        copy.start()
+    finish(k)
 
     def sent(when, copies):
         @pl.when(when)
@@ -397,7 +408,7 @@
     sent(cross_u, send_gr)
     sent(fold, send_gfold)
     sent(relay_g, pass_g)
-    for copy in saves(0) + saves(1) + last:
+    for copy in saves(0) + saves(1) + last(0) + last(1):
         copy.wait()
 
 
@@ -446,6 +457,8 @@
             pltpu.VMEM((2, 3 * CH, HD), f32),
             pltpu.VMEM((3, WIN, QH * SUB), bf16),
             pltpu.VMEM((3, 8, QH * SUB), f32),
+            pltpu.VMEM((3, WIN, SUB), f32),
+            pltpu.VMEM((3, HD, QH * SUB), bf16),
             pltpu.VMEM((3, HD, QH * SUB), bf16),
             pltpu.VMEM((3, HD, QH * SUB), f32),
             pltpu.VMEM((2, 2, 2 * CH, HD), bf16),
@@ -457,7 +470,7 @@
             pltpu.SemaphoreType.DMA((COPIES,)),
             pltpu.SemaphoreType.DMA((4,)),
             pltpu.SemaphoreType.DMA((6,)),
-            pltpu.SemaphoreType.DMA((6,)),
+            pltpu.SemaphoreType.DMA((8,)),
         ],
         compiler_params=pltpu.CompilerParams(
             collective_id=0, has_side_effects=True, vmem_limit_bytes=60_000_000

time: 56.2 us -> 56.2 us (level)
  no operation moved by 1% of the time
where the time goes in v4:
time: 56.2 us; the launch traced here: 56 us
  Pallas kernels  55.4 us (99%)
  between operations  0.64 us (1%)
    pallas_call x1, Pallas kernels, body(): pl.pallas_call(kernel, out_shape=shapes, in_specs=[hbm] * 4 + [vmem], out...  52.9 us
    pallas_call x1, Pallas kernels, body(): pl.pallas_call(write, out_shape=shapes, in_specs=[hbm] * 4, out_specs=[hb...  2.46 us

profile of v4, /device:TPU:199, one launch (start us, length us, event | category | flops | bytes accessed | tf_op | source)
XLA Modules:
  0.0 56.0 jit_solution(7228010739243952920)
XLA Ops:
  0.6 52.9 %shard_map.84 = (bf16[768,512]{1,0:T(8,128)(2,1)}, bf16[768,512]{1,0:T(8,128)(2,1)}, bf16[768,128]{1,0:T(8,128)(2,1)}, bf16[768,128]{1,0:T(8,128)(2,1)}) custom-call(bf16[768,512]{1,0:T(8,128)(2,1)} %q_hbm.1, bf16[768,128]{1,0:T(8,128)(2,1)} %k_hbm.1, bf16[768,128]{1,0:T(8,128)(2,1)} %v_hbm.1, bf16[768,512]{1,0:T(8,128)(2,1)} %do_hbm.1, s32[1,128]{1,0:T(1,128)} %bitcast.1), custom_call_target="tpu_custom_call" | custom-call | flops 4300000256 | bytes 4000000 | tf_op jit(solution)/shard_map/pallas_call | solution.py:445
  53.5 2.5 %shard_map.85 = (bf16[768,512]{1,0:T(8,128)(2,1)}, bf16[768,512]{1,0:T(8,128)(2,1)}, bf16[768,128]{1,0:T(8,128)(2,1)}, bf16[768,128]{1,0:T(8,128)(2,1)}) custom-call(bf16[768,512]{1,0:T(8,128)(2,1)} %get-tuple-element.8.refs_0_, bf16[768,512]{1,0:T(8,128)(2,1)} %get-tuple-element.9.refs_1_, bf16[768,128]{1,0:T(8,128)(2,1)} %get-tuple-element.10.refs_2_, ...), custom_call_target="tpu_custom_call" | custom-call | bytes 4000000 | tf_op jit(solution)/shard_map/pallas_call | solution.py:482
